TPU v7x, 32 devices: a whole 2x2x4 slice. The times are simulated.
32 devices in a mesh: grp: 8 (over z, core), dev: 4 (over y, x).
Axes of the slice: x: 2, y: 2, z: 4, core: 2. Of those that a mesh axis runs over, the one named last changes fastest.
Arguments:
- residual: bfloat16 [128, 7168], P(('grp', 'dev')), may hold values from -6 to 6
- routes: int32 [128, 2], P(('grp', 'dev')), may hold values from 0 to 3, all different within a row; in each aligned block of 4 rows (0 to 3, 4 to 7, ...) at most 3 rows name the same one
- gate_weights: bfloat16 [128, 2], P(('grp', 'dev')), may hold values from 0.19921875 to 1.5
- moe_gain: bfloat16 [7168], replicated, may hold values from 0.25 to 1.75
- attn_gain: bfloat16 [7168], replicated, may hold values from 0.25 to 1.75
- kv_gain: bfloat16 [512], replicated, may hold values from 0.25 to 1.75
- w_gate: bfloat16 [7168, 4096], P(None, 'dev'), may hold values from -0.0625 to 0.0625
- w_up: bfloat16 [7168, 4096], P(None, 'dev'), may hold values from -0.0625 to 0.0625
- w_down: bfloat16 [4096, 7168], P('dev'), may hold values from -0.1875 to 0.1875
- w_kv: bfloat16 [7168, 576], P('grp'), may hold values from -0.0625 to 0.0625
- q_lat: bfloat16 [128, 64, 512], P(('grp', 'dev')), may hold values from -24 to 24
- q_rope: bfloat16 [128, 64, 64], P(('grp', 'dev')), may hold values from -24 to 24
- cache_lat: bfloat16 [384, 128, 512], P(('grp', 'dev')), may hold values from -12 to 12
- cache_rope: bfloat16 [384, 64, 128], P(('grp', 'dev')), may hold values from -12 to 12
- page_table: int32 [128, 4], P(('grp', 'dev')), may hold values from 0 to 11, as said below
- lengths: int32 [128], P(('grp', 'dev')), may hold values from 1 to 511
Outputs:
- residual_next: bfloat16 [128, 7168], P(('grp', 'dev'))
- new_entry: bfloat16 [128, 576], P(('grp', 'dev'))
- attn_out: bfloat16 [128, 64, 512], P(('grp', 'dev'))
Inputs may be any that keep to these rules, and one draw needn't show every extreme that they name: In the 4 rows of one device no expert is named by more than 3 routes. `page_table`: entries are pages of the pool of the request's own device; the requests of one device share their first page.
All inputs are finite; a program needn't handle non-finite values.
Results may differ from a plain program's by a relative error of at most 0.0068.
Values may be sent and summed in bfloat16 or wider, within the bound.
A program may use at most 128 MiB of HBM per device.

v0:
```python
import jax
import jax.numpy as jnp
from jax import lax
from jax.sharding import PartitionSpec as P

HEADS = 64
LAT = 512
ROPE = 64
EXPERTS = 4
TOP = 2
PAGE = 128
PAGES_REQ = 4
CAP = 3


epsilon = 1e-06
score_scale = 192.0 ** (-0.5)


def rms_scale(values, gain):
    widened = values.astype(jnp.float32)
    return (
        widened
        * lax.rsqrt(jnp.mean(widened * widened, axis=-1, keepdims=True) + epsilon)
        * gain.astype(jnp.float32)
    )


def expert_part(picked_rows, w_gate, w_up, w_down):
    gate_proj = jnp.dot(picked_rows, w_gate, preferred_element_type=jnp.float32)
    up_proj = jnp.dot(picked_rows, w_up, preferred_element_type=jnp.float32)
    hidden = (jax.nn.silu(gate_proj) * up_proj).astype(jnp.bfloat16)
    return jnp.dot(hidden, w_down, preferred_element_type=jnp.float32).astype(jnp.bfloat16)


def new_key(kv_rows, kv_gain, lengths):
    latent = rms_scale(kv_rows[:, :LAT], kv_gain)
    half_width = ROPE // 2
    freqs = 10000.0 ** (-(2.0 * jnp.arange(half_width, dtype=jnp.float32)) / ROPE)
    angle = lengths.astype(jnp.float32)[:, None] * freqs[None, :]
    first_half = kv_rows[:, LAT : LAT + half_width]
    second_half = kv_rows[:, LAT + half_width :]
    rotated = jnp.concatenate(
        [
            first_half * jnp.cos(angle) - second_half * jnp.sin(angle),
            second_half * jnp.cos(angle) + first_half * jnp.sin(angle),
        ],
        axis=1,
    )
    return jnp.concatenate([latent, rotated], axis=1).astype(jnp.bfloat16)


def attend(q_lat, q_rope, cache_lat, cache_rope, page_table, lengths, new_entry):
    token_count = q_lat.shape[0]
    key_span = PAGES_REQ * PAGE
    keys_lat = cache_lat[page_table].reshape(token_count, key_span, LAT)
    keys_rope = cache_rope[page_table]
    score_lat = jnp.einsum("thc,tlc->thl", q_lat, keys_lat, preferred_element_type=jnp.float32)
    score_rope = jnp.einsum(
        "thr,tpru->thpu", q_rope, keys_rope, preferred_element_type=jnp.float32
    ).reshape(token_count, HEADS, key_span)
    scores = (score_lat + score_rope) * score_scale
    new_lat = new_entry[:, :LAT]
    new_rope = new_entry[:, LAT:]
    self_score = (
        jnp.einsum("thc,tc->th", q_lat, new_lat, preferred_element_type=jnp.float32)
        + jnp.einsum("thr,tr->th", q_rope, new_rope, preferred_element_type=jnp.float32)
    ) * score_scale
    live_mask = (jnp.arange(key_span, dtype=jnp.int32)[None, :] < lengths[:, None])[:, None, :]
    masked = jnp.where(live_mask, scores, -1e30)
    largest = jnp.maximum(jnp.max(masked, axis=2), self_score)
    exps = jnp.where(live_mask, jnp.exp(masked - largest[:, :, None]), 0.0)
    self_exp = jnp.exp(self_score - largest)
    total = jnp.sum(exps, axis=2) + self_exp
    summed = jnp.einsum(
        "thl,tlc->thc", exps.astype(jnp.bfloat16), keys_lat, preferred_element_type=jnp.float32
    )
    self_prob = lax.optimization_barrier(self_exp.astype(jnp.bfloat16)).astype(jnp.float32)
    summed = summed + self_prob[:, :, None] * new_lat.astype(jnp.float32)[:, None, :]
    return (summed / total[:, :, None]).astype(jnp.bfloat16)


def local(
    residual,
    routes,
    gate_weights,
    moe_gain,
    attn_gain,
    kv_gain,
    w_gate,
    w_up,
    w_down,
    w_kv,
    q_lat,
    q_rope,
    cache_lat,
    cache_rope,
    page_table,
    lengths,
):
    token_count = residual.shape[0]
    moe_in = rms_scale(residual, moe_gain).astype(jnp.bfloat16)
    group_size = lax.axis_size("dev")
    shards = group_size // EXPERTS
    expert_ids = jnp.arange(EXPERTS, dtype=jnp.int32)
    flat_routes = routes.reshape(-1)
    onehot = (flat_routes[:, None] == expert_ids[None, :]).astype(jnp.int32)
    slot_index = jnp.sum((jnp.cumsum(onehot, axis=0) - onehot) * onehot, axis=1)
    picked = (
        (flat_routes[None, None, :] == expert_ids[:, None, None])
        & (slot_index[None, None, :] == jnp.arange(CAP, dtype=jnp.int32)[None, :, None])
    ).astype(jnp.float32)
    picked = picked.reshape(EXPERTS, CAP, token_count, TOP)
    placing = jnp.sum(picked, axis=3).astype(jnp.bfloat16)
    per_expert = jnp.einsum(
        "ect,td->ecd", placing, moe_in, preferred_element_type=jnp.float32
    ).astype(jnp.bfloat16)
    outgoing = jnp.repeat(per_expert, shards, axis=0)
    arrived = lax.all_to_all(outgoing, "dev", split_axis=0, concat_axis=0, tiled=True)
    sources, slot_count, feature_width = arrived.shape
    expert_rows = expert_part(
        arrived.reshape(sources * slot_count, feature_width), w_gate, w_up, w_down
    )
    returned = lax.all_to_all(
        expert_rows.reshape(sources, slot_count, feature_width),
        "dev",
        split_axis=0,
        concat_axis=0,
        tiled=True,
    )
    shard_sums = jnp.sum(returned.astype(jnp.float32).reshape(EXPERTS, shards, CAP, -1), axis=1)
    combine = jnp.einsum(
        "ectk,tk->tec", picked, gate_weights.astype(jnp.float32), precision=lax.Precision.HIGHEST
    )
    moe_out = jnp.einsum("tec,ecd->td", combine, shard_sums, precision=lax.Precision.HIGHEST)
    residual_next = (residual.astype(jnp.float32) + moe_out).astype(jnp.bfloat16)
    attn_in = rms_scale(residual_next, attn_gain).astype(jnp.bfloat16)
    column_rows = lax.all_to_all(attn_in, "grp", split_axis=1, concat_axis=0, tiled=True)
    kv_rows = lax.psum_scatter(
        jnp.dot(column_rows, w_kv, preferred_element_type=jnp.float32),
        "grp",
        scatter_dimension=0,
        tiled=True,
    )
    new_entry = new_key(kv_rows, kv_gain, lengths)
    attn_out = attend(q_lat, q_rope, cache_lat, cache_rope, page_table, lengths, new_entry)
    return (residual_next, new_entry, attn_out)


def solution(mesh):
    in_specs = (
        P(("grp", "dev"), None),
        P(("grp", "dev"), None),
        P(("grp", "dev"), None),
        P(),
        P(),
        P(),
        P(None, "dev"),
        P(None, "dev"),
        P("dev", None),
        P("grp", None),
        P(("grp", "dev"), None, None),
        P(("grp", "dev"), None, None),
        P(("grp", "dev"), None, None),
        P(("grp", "dev"), None, None),
        P(("grp", "dev"), None),
        P(("grp", "dev")),
    )
    out_specs = (P(("grp", "dev"), None), P(("grp", "dev"), None), P(("grp", "dev"), None, None))
    return jax.shard_map(local, mesh=mesh, in_specs=in_specs, out_specs=out_specs, check_vma=False)
```

profile of v0, /device:TPU:8, one launch (start us, length us, event | category | flops | bytes accessed | tf_op | source)
XLA Modules:
  0.0 130.4 jit_solution(649244028120999096)
XLA Ops:
  7.2 0.0 copy-start
  7.2 0.8 iota_compare_fusion.1
  8.0 0.8 copy.35
  8.7 1.0 fusion.18
  9.7 0.1 eq.56
  9.8 0.2 reduce_window_sum.11
  10.0 0.1 eq.60
  10.1 0.1 copy.36
  10.2 0.7 convert_element_type.69
  11.0 1.1 convolution_convert_fusion.1
  12.1 0.8 copy.37
  12.9 3.7 %all-to-all-start = ((bf16[4,3,7168]{2,1,0:T(4,128)(2,1)}), bf16[4,3,7168]{2,1,0:T(4,128)(2,1)S(1)}, u32[]{:S(2)}, u32[]{:S(2)}) async-start(bf16[4,3,7168]{2,1,0:T(4,128)(2,1)} %copy.37), calls=%async_computation | async-start | bytes 458752 | tf_op jit(solution)/shard_map/all_to_all | solution.py:119
  16.6 0.7 compare_select_fusion
  17.3 0.7 iota_compare_fusion
  18.0 0.7 convert.11
  18.7 0.1 reshape.147
  18.8 3.1 %all-to-all-done = bf16[4,3,7168]{2,1,0:T(4,128)(2,1)S(1)} async-done(((bf16[4,3,7168]{2,1,0:T(4,128)(2,1)}), bf16[4,3,7168]{2,1,0:T(4,128)(2,1)S(1)}, u32[]{:S(2)}, u32[]{:S(2)}) %all-to-all-start) | async-done | bytes 172064 | tf_op jit(solution)/shard_map/all_to_all | solution.py:119
  21.9 0.2 reshape.141
  22.0 7.2 %fusion.54 = f32[12,1024]{1,0:T(8,128)S(1)} fusion(bf16[12,7168]{1,0:T(8,128)(2,1)S(1)} %reshape.141, bf16[7168,1024]{1,0:T(8,128)(2,1)} %param.22), kind=kOutput, calls=%fused_computation.88 | convolution fusion | flops 176160768 | bytes 14901248 | tf_op jit(solution)/shard_map/dot_general | solution.py:30
  29.2 0.0 copy-start.6
  29.2 0.0 copy-start.1
  29.2 0.0 copy-start.4
  29.2 0.0 copy-start.3
  29.2 0.0 copy-start.2
  29.2 0.0 copy-start.8
  29.3 0.0 copy-start.7
  29.3 0.0 copy-start.9
  29.3 13.4 %convolution_convert_fusion = bf16[12,7168]{1,0:T(8,128)(2,1)S(1)} fusion(bf16[1024,7168]{1,0:T(8,128)(2,1)} %param.24, bf16[12,7168]{1,0:T(8,128)(2,1)S(1)} %reshape.141, bf16[7168,1024]{1,0:T(8,128)(2,1)} %param.23, f32[12,1024]{1,0:T(8,128)S(1)} %fusion.54), kind=kOutput, calls=%fused_computation.2 | convolution fusion | flops 352481280 | bytes 29753344 | tf_op jit(solution)/shard_map/dot_general | solution.py:33
  42.6 0.8 reshape.142
  43.5 3.4 %all-to-all-start.1 = ((bf16[4,3,7168]{2,1,0:T(4,128)(2,1)}), bf16[4,3,7168]{2,1,0:T(4,128)(2,1)S(1)}, u32[]{:S(2)}, u32[]{:S(2)}) async-start(bf16[4,3,7168]{2,1,0:T(4,128)(2,1)} %reshape.142), calls=%async_computation.1 | async-start | bytes 458752 | tf_op jit(solution)/shard_map/all_to_all | solution.py:124
  46.9 0.0 copy-done.6
  46.9 0.0 copy-done.1
  46.9 0.6 gather_fusion.1
  47.5 0.0 copy-done
  47.5 2.0 %gather_fusion = bf16[16,128,512]{2,1,0:T(8,128)(2,1)} fusion(bf16[12,128,512]{2,1,0:T(8,128)(2,1)S(1)} %copy-done, s32[1024]{0:T(1024)S(1)} %pad_clamp_fusion), kind=kCustom, calls=%fused_computation | custom fusion | bytes 4194368 | tf_op jit(solution)/shard_map/gather | solution.py:56
  49.5 0.0 copy-done.4
  49.5 0.2 convolution_bitcast_fusion.1
  49.8 2.3 %all-to-all-done.1 = bf16[4,3,7168]{2,1,0:T(4,128)(2,1)S(1)} async-done(((bf16[4,3,7168]{2,1,0:T(4,128)(2,1)}), bf16[4,3,7168]{2,1,0:T(4,128)(2,1)S(1)}, u32[]{:S(2)}, u32[]{:S(2)}) %all-to-all-start.1) | async-done | bytes 172064 | tf_op jit(solution)/shard_map/all_to_all | solution.py:124
  52.1 0.0 copy-done.3
  52.1 0.5 fusion.15
  52.6 0.0 copy-start.5
  52.7 0.7 fusion.17
  53.4 5.3 %all-to-all-start.2 = ((bf16[4,8,896]{2,0,1:T(4,128)(2,1)}), bf16[4,8,896]{2,0,1:T(4,128)(2,1)S(1)}, u32[]{:S(2)}, u32[]{:S(2)}) async-start(bf16[4,8,896]{2,0,1:T(4,128)(2,1)} %bitcast.3), calls=%async_computation.2 | async-start | bytes 114688 | tf_op jit(solution)/shard_map/all_to_all | solution.py:138
  58.7 0.0 all-reduce.3.cloned.1.call-start
  58.7 0.0 copy-done.2
  58.7 2.4 %fusion.53 = (f32[4,64]{1,0:T(4,128)S(1)}, f32[4,64,512]{2,1,0:T(8,128)S(1)}) fusion(f32[4,4,8,8,128]{4,3,2,1,0:T(8,128)S(1)} %convolution_bitcast_fusion.1, bf16[4,512,512]{2,1,0:T(8,128)(2,1)} %bitcast.58, bf16[4,64,512]{2,1,0:T(8,128)(2,1)S(1)} %copy-done.2, pred[4,512]{1,0:T(4,128)(4,1)S(1)} %iota_compare_fusion), kind=kOutput, calls=%fused_computation.87 | convolution fusion | flops 134741760 | bytes 3410944 | tf_op jit(solution)/shard_map/thc,tlc->thl/dot_general | solution.py:58
  61.1 2.1 %all-to-all-done.2 = bf16[4,8,896]{2,0,1:T(4,128)(2,1)S(1)} async-done(((bf16[4,8,896]{2,0,1:T(4,128)(2,1)}), bf16[4,8,896]{2,0,1:T(4,128)(2,1)S(1)}, u32[]{:S(2)}, u32[]{:S(2)}) %all-to-all-start.2) | async-done | bytes 57376 | tf_op jit(solution)/shard_map/all_to_all | solution.py:138
  63.3 2.3 %fusion.55 = f32[32,576]{1,0:T(8,128)} fusion(bf16[32,896]{1,0:T(8,128)(2,1)S(1)} %all_to_all.25, bf16[896,576]{0,1:T(8,128)(2,1)} %param.25), kind=kOutput, calls=%fused_computation.89 | convolution fusion | flops 33030144 | bytes 1163264 | tf_op jit(solution)/shard_map/dot_general | solution.py:140
  65.6 0.0 all-reduce.3.cloned.1.call-update
  65.6 0.0 copy-done.8
  65.6 0.0 copy-done.7
  65.7 0.0 copy-done.9
  65.7 0.6 dynamic-slice
  66.9 49.9 %all-reduce.3.cloned.1.call-done = f32[32,576]{1,0:T(8,128)} async-done(((f32[32,576]{1,0:T(8,128)}), f32[32,576]{1,0:T(8,128)}) %all-reduce.3.cloned.1.call-update) | async-done | bytes 73744
  116.9 0.8 multiply_reduce_fusion
  117.7 0.9 fusion.41
  118.6 0.1 maximum_bitcast_fusion
  118.7 0.1 fusion.44
  118.8 0.8 fusion.52
  119.6 0.7 pad_maximum_fusion
  120.3 0.2 fusion.33
  120.5 0.2 fusion.8
  120.7 2.8 %fusion.6 = bf16[4,64,512]{2,1,0:T(8,128)(2,1)} fusion(bf16[4,512,512]{2,1,0:T(8,128)(2,1)} %bitcast.59, f32[4,64,512]{2,1,0:T(8,128)S(1)} %get-tuple-element.12, f32[4,64]{1,0:T(4,128)S(1)} %get-tuple-element.8, f32[4,512]{1,0:T(4,128)S(1)} %get-tuple-element.3, f32[4,64]{1,0:T(4,128)S(1)} %convert_element_type.82, f32[4,64]{1,0:T(4,128)S(1)} %fusion.47, ...), kind=kOutput, calls=%fused_computation.14 | convolution fusion | flops 135135232 | bytes 2896896 | tf_op jit(solution)/shard_map/thl,tlc->thc/dot_general | solution.py:75
  123.6 0.0 copy-done.5
  (17 shorter events, 0.2 us)
Async XLA Ops:
  7.2 40.3 %copy-start = (bf16[12,128,512]{2,1,0:T(8,128)(2,1)S(1)}, bf16[12,128,512]{2,1,0:T(8,128)(2,1)}, u32[]{:S(2)}) copy-start(bf16[12,128,512]{2,1,0:T(8,128)(2,1)} %param.28) | copy-start | bytes 4718596
  12.9 9.0 %all-to-all-start = ((bf16[4,3,7168]{2,1,0:T(4,128)(2,1)}), bf16[4,3,7168]{2,1,0:T(4,128)(2,1)S(1)}, u32[]{:S(2)}, u32[]{:S(2)}) async-start(bf16[4,3,7168]{2,1,0:T(4,128)(2,1)} %copy.37), calls=%async_computation | async-start | bytes 458752 | tf_op jit(solution)/shard_map/all_to_all | solution.py:119
  29.2 17.7 %copy-start.6 = (bf16[7168]{0:T(1024)(128)(2,1)S(1)}, bf16[7168]{0:T(1024)(128)(2,1)}, u32[]{:S(2)}) copy-start(bf16[7168]{0:T(1024)(128)(2,1)} %param.20) | copy-start | bytes 43012
  29.2 17.7 %copy-start.1 = (bf16[12,64,128]{2,1,0:T(8,128)(2,1)S(1)}, bf16[12,64,128]{2,1,0:T(8,128)(2,1)}, u32[]{:S(2)}) copy-start(bf16[12,64,128]{2,1,0:T(8,128)(2,1)} %param.29) | copy-start | bytes 589828
  29.2 20.3 %copy-start.4 = (bf16[4,64,64]{2,1,0:T(8,128)(2,1)S(1)}, bf16[4,64,64]{2,1,0:T(8,128)(2,1)}, u32[]{:S(2)}) copy-start(bf16[4,64,64]{2,1,0:T(8,128)(2,1)} %param.27) | copy-start | bytes 98308
  29.2 22.9 %copy-start.3 = (bf16[4,7168]{1,0:T(4,128)(2,1)S(1)}, bf16[4,7168]{1,0:T(4,128)(2,1)}, u32[]{:S(2)}) copy-start(bf16[4,7168]{1,0:T(4,128)(2,1)} %param.16) | copy-start | bytes 172036
  29.2 29.5 %copy-start.2 = (bf16[4,64,512]{2,1,0:T(8,128)(2,1)S(1)}, bf16[4,64,512]{2,1,0:T(8,128)(2,1)}, u32[]{:S(2)}) copy-start(bf16[4,64,512]{2,1,0:T(8,128)(2,1)} %param.26) | copy-start | bytes 786436
  29.2 36.4 %copy-start.8 = (s32[4]{0:T(128)S(1)}, s32[4]{0:T(128)}, u32[]{:S(2)}) copy-start(s32[4]{0:T(128)} %param.31) | copy-start | bytes 52
  29.3 36.4 %copy-start.7 = (bf16[512]{0:T(512)(128)(2,1)S(1)}, bf16[512]{0:T(512)(128)(2,1)}, u32[]{:S(2)}) copy-start(bf16[512]{0:T(512)(128)(2,1)} %param.21) | copy-start | bytes 3076
  29.3 36.4 %copy-start.9 = (u32[32]{0:T(128)S(1)}, u32[32]{0:T(128)}, u32[]{:S(2)}) copy-start(u32[32]{0:T(128)} %constant.50) | copy-start | bytes 388
  43.5 8.6 %all-to-all-start.1 = ((bf16[4,3,7168]{2,1,0:T(4,128)(2,1)}), bf16[4,3,7168]{2,1,0:T(4,128)(2,1)S(1)}, u32[]{:S(2)}, u32[]{:S(2)}) async-start(bf16[4,3,7168]{2,1,0:T(4,128)(2,1)} %reshape.142), calls=%async_computation.1 | async-start | bytes 458752 | tf_op jit(solution)/shard_map/all_to_all | solution.py:124
  52.6 70.9 %copy-start.5 = (bf16[4,7168]{1,0:T(4,128)(2,1)}, bf16[4,7168]{1,0:T(4,128)(2,1)S(1)}, u32[]{:S(2)}) copy-start(bf16[4,7168]{1,0:T(4,128)(2,1)S(1)} %get-tuple-element.10) | copy-start | bytes 172036
  53.4 9.9 %all-to-all-start.2 = ((bf16[4,8,896]{2,0,1:T(4,128)(2,1)}), bf16[4,8,896]{2,0,1:T(4,128)(2,1)S(1)}, u32[]{:S(2)}, u32[]{:S(2)}) async-start(bf16[4,8,896]{2,0,1:T(4,128)(2,1)} %bitcast.3), calls=%async_computation.2 | async-start | bytes 114688 | tf_op jit(solution)/shard_map/all_to_all | solution.py:138
  58.7 58.2 %all-reduce.3.cloned.1.call-start = ((), (), s32[]{:S(2)}) async-start(), calls=%async_computation.3 | async-start | bytes 163840
Sparse Core Ops, SparseCore 0:
  65.7 51.0 all-reduce.2
where the time goes:
time: 131 us; the launch traced here: 130 us
  waiting for transfers between devices  57.5 us (44%)
  matrix products  30.2 us (23%)
  between operations  14.9 us (11%)
  starting transfers between devices  12.4 us (9%)
  other arithmetic  9.16 us (7%)
  local copies, waits for them, and re-layouts  6.17 us (5%)
    unnamed x2, waiting for transfers between devices  50 us
    dot_general x1, matrix products, expert_part(): jnp.dot(hidden, w_down, preferred_element_type=jnp.float32)  13.4 us
    dot_general x1, matrix products, expert_part(): gate_proj = jnp.dot(picked_rows, w_gate, preferred_element_type=jnp.float32)  7.17 us
    all_to_all x1, starting transfers between devices, local(): lax.all_to_all(attn_in, 'grp', split_axis=1, concat_axis=0, tiled=True)  5.32 us
    all_to_all x1, starting transfers between devices, local(): lax.all_to_all(outgoing, 'dev', split_axis=0, concat_axis=0, tiled=True)  3.72 us
    all_to_all x1, starting transfers between devices, local(): lax.all_to_all(expert_rows.reshape(sources, slot_count, feature_width), '...  3.39 us
    all_to_all x1, waiting for transfers between devices, local(): lax.all_to_all(outgoing, 'dev', split_axis=0, concat_axis=0, tiled=True)  3.11 us
    dot_general x1, matrix products, attend(): jnp.einsum('thl,tlc->thc', exps.astype(jnp.bfloat16), keys_lat, preferred...  2.83 us
  transfers between devices with their start and end apart: 4, of which 4 were waited for; matrix products, arithmetic and copies ran while one was open for 6% of the time, Pallas kernels for 0%

commit v1 on v0

--- a/solution.py
+++ b/solution.py
@@ -1,8 +1,14 @@
+import functools
+import math
+
 import jax
 import jax.numpy as jnp
 from jax import lax
+from jax.experimental import pallas as pl
+from jax.experimental.pallas import tpu as pltpu
 from jax.sharding import PartitionSpec as P
 
+WIDTH = 7168
 HEADS = 64
 LAT = 512
 ROPE = 64
@@ -147,7 +153,570 @@
     return (residual_next, new_entry, attn_out)
 
 
+def fused_kernel(
+    group_count,
+    dev_count,
+    residual_ref,
+    routes_ref,
+    gates_ref,
+    moe_gain_ref,
+    attn_gain_ref,
+    kv_gain_ref,
+    lengths_ref,
+    lengths_smem,
+    table_smem,
+    w_gate_hbm,
+    w_up_hbm,
+    w_down_hbm,
+    w_kv_hbm,
+    q_lat_hbm,
+    q_rope_hbm,
+    cache_lat_hbm,
+    cache_rope_hbm,
+    out_residual,
+    out_entry,
+    out_attn,
+    w_gate,
+    w_up,
+    w_down,
+    w_kv,
+    q_lat,
+    q_rope,
+    cache_lat,
+    cache_rope,
+    pack32,
+    disp_send,
+    disp_recv,
+    rows32,
+    rows16,
+    gate_acc,
+    up_acc,
+    hidden,
+    combine,
+    residual_pack,
+    gain_pack,
+    next_pack,
+    square_acc,
+    ret_send,
+    ret_recv,
+    col_send,
+    col_recv,
+    col32,
+    part_send,
+    part_recv,
+    attn_acc,
+    attn_max,
+    attn_sum,
+    rope_cos,
+    rope_sin,
+    next32,
+    load_sem,
+    gate_sem,
+    up_sem,
+    down_sem,
+    disp_send_sem,
+    disp_recv_sem,
+    ret_send_sem,
+    ret_recv_sem,
+    col_send_sem,
+    col_recv_sem,
+    part_send_sem,
+    part_recv_sem,
+):
+    f32 = jnp.float32
+    bf16 = jnp.bfloat16
+    me_g = lax.axis_index("grp")
+    me_d = lax.axis_index("dev")
+    tokens, width = residual_ref.shape
+    quarter = width // 4
+    chunks = group_count // 2
+    block = width // group_count
+    k_chunks, k_rows, _ = w_gate.shape
+    down_cols = width // chunks
+    pack_width = col_send.shape[-1]
+    widths = [min(pack_width, block - q * pack_width) for q in range(4)]
+
+    def remote(src, dst, send, recv, grp, dev):
+        return pltpu.make_async_remote_copy(
+            src_ref=src,
+            dst_ref=dst,
+            send_sem=send,
+            recv_sem=recv,
+            device_id=(grp, dev),
+            device_id_type=pl.DeviceIdType.MESH,
+        )
+
+    barrier = pltpu.get_barrier_semaphore()
+    for r in range(1, dev_count):
+        pl.semaphore_signal(
+            barrier,
+            inc=1,
+            device_id=(me_g, lax.rem(me_d + r, dev_count)),
+            device_id_type=pl.DeviceIdType.MESH,
+        )
+    for r in range(1, group_count):
+        pl.semaphore_signal(
+            barrier,
+            inc=1,
+            device_id=(lax.rem(me_g + r, group_count), me_d),
+            device_id_type=pl.DeviceIdType.MESH,
+        )
+
+    loads = [
+        pltpu.make_async_copy(src, dst, load_sem.at[at])
+        for at, (src, dst) in enumerate(
+            [
+                (q_lat_hbm, q_lat),
+                (q_rope_hbm, q_rope),
+                (cache_lat_hbm, cache_lat),
+                (cache_rope_hbm, cache_rope),
+                (w_kv_hbm, w_kv),
+            ]
+        )
+    ]
+    for load in loads[:4]:
+        load.start()
+
+    def gate_copy(k):
+        return pltpu.make_async_copy(
+            w_gate_hbm.at[pl.ds(k * k_rows, k_rows), :], w_gate.at[k], gate_sem.at[k]
+        )
+
+    def up_copy(k):
+        return pltpu.make_async_copy(
+            w_up_hbm.at[pl.ds(k * k_rows, k_rows), :], w_up.at[k], up_sem.at[k]
+        )
+
+    def chunk_at(step):
+        return lax.rem(me_g // 2 + 1 + step, chunks)
+
+    def down_copy(step):
+        start = pl.multiple_of(chunk_at(step) * down_cols, 128)
+        return pltpu.make_async_copy(
+            w_down_hbm.at[:, pl.ds(start, down_cols)], w_down.at[step], down_sem.at[step]
+        )
+
+    for k in range(k_chunks):
+        gate_copy(k).start()
+        up_copy(k).start()
+    for step in range(chunks):
+        down_copy(step).start()
+    loads[4].start()
+
+    residual = residual_ref[...].astype(f32)
+    moe_in = (
+        residual
+        * lax.rsqrt(jnp.mean(residual * residual, axis=1, keepdims=True) + epsilon)
+        * moe_gain_ref[...].astype(f32)
+    )
+    for q in range(4):
+        pack32[tokens * q : tokens * (q + 1), :] = moe_in[:, q * quarter : (q + 1) * quarter]
+    packed = pack32[...].astype(bf16)
+    disp_send[...] = packed
+    disp_recv[me_d] = packed
+
+    pl.semaphore_wait(barrier, dev_count - 1 + group_count - 1)
+
+    def disp_copy(r):
+        dest = lax.rem(me_d + r, dev_count)
+        return remote(
+            disp_send, disp_recv.at[me_d], disp_send_sem.at[r], disp_recv_sem.at[me_d], me_g, dest
+        )
+
+    for r in range(1, dev_count):
+        disp_copy(r).start()
+
+    routes = routes_ref[...]
+    gates = gates_ref[...].astype(f32)
+    for e in range(dev_count):
+        weight = jnp.sum(jnp.where(routes == e, gates, 0.0), axis=1, keepdims=True)
+        weight = jnp.broadcast_to(weight, (tokens, 128))
+        for q in range(4):
+            combine[e, tokens * q : tokens * (q + 1), :] = weight
+    residual_pack[...] = jnp.zeros_like(residual_pack)
+    gain_pack[...] = jnp.zeros_like(gain_pack)
+    attn_gain = attn_gain_ref[...].astype(f32)
+    for g in range(group_count):
+        for q in range(4):
+            rows = slice(tokens * q, tokens * (q + 1))
+            start = g * block + q * pack_width
+            residual_pack[g, rows, : widths[q]] = residual[:, start : start + widths[q]]
+            gain_pack[g, rows, : widths[q]] = jnp.broadcast_to(
+                attn_gain[:, start : start + widths[q]], (tokens, widths[q])
+            )
+    square_acc[...] = jnp.zeros_like(square_acc)
+    half_width = ROPE // 2
+    at = lax.broadcasted_iota(jnp.int32, (tokens, half_width), 1).astype(f32)
+    freqs = jnp.exp(at * (-2.0 / ROPE * math.log(10000.0)))
+    angle = lengths_ref[...].astype(f32) * freqs
+    rope_cos[...] = jnp.cos(angle)
+    rope_sin[...] = jnp.sin(angle)
+
+    for load in loads[:4]:
+        load.wait()
+    for t in range(tokens):
+        query = q_lat[t]
+        query_rope = q_rope[t]
+        pages = [cache_lat[table_smem[t, p]] for p in range(PAGES_REQ)]
+        scores = []
+        for p in range(PAGES_REQ):
+            rope_page = cache_rope[table_smem[t, p]]
+            scores.append(
+                lax.dot_general(
+                    query, pages[p], (((1,), (1,)), ((), ())), preferred_element_type=f32
+                )
+                + jnp.dot(query_rope, rope_page, preferred_element_type=f32)
+            )
+        scores = jnp.concatenate(scores, axis=1) * score_scale
+        live = lax.broadcasted_iota(jnp.int32, scores.shape, 1) < lengths_smem[t]
+        masked = jnp.where(live, scores, -1e30)
+        largest = jnp.max(masked, axis=1, keepdims=True)
+        exps = jnp.where(live, jnp.exp(masked - largest), 0.0)
+        attn_max[t] = largest
+        attn_sum[t] = jnp.sum(exps, axis=1, keepdims=True)
+        probs = exps.astype(bf16)
+        summed = jnp.zeros((HEADS, LAT), f32)
+        for p in range(PAGES_REQ):
+            summed = summed + jnp.dot(
+                probs[:, p * PAGE : (p + 1) * PAGE], pages[p], preferred_element_type=f32
+            )
+        attn_acc[t] = summed
+
+    for r in range(1, dev_count):
+        source = lax.rem(me_d + r, dev_count)
+        remote(
+            disp_send, disp_recv.at[source], disp_send_sem.at[r], disp_recv_sem.at[source], me_g, source
+        ).wait_recv()
+    for s in range(dev_count):
+        part = disp_recv[s].astype(f32)
+        for q in range(4):
+            rows32[tokens * s : tokens * (s + 1), q * quarter : (q + 1) * quarter] = part[
+                tokens * q : tokens * (q + 1), :
+            ]
+    for k in range(k_chunks):
+        rows16[k] = rows32[:, k * k_rows : (k + 1) * k_rows].astype(bf16)
+
+    gate_acc[...] = jnp.zeros_like(gate_acc)
+    up_acc[...] = jnp.zeros_like(up_acc)
+
+    @pl.loop(0, k_chunks)
+    def _(k):
+        gate_copy(k).wait()
+        picked = rows16[k]
+        gate_acc[...] += jnp.dot(picked, w_gate[k], preferred_element_type=f32)
+        up_copy(k).wait()
+        up_acc[...] += jnp.dot(picked, w_up[k], preferred_element_type=f32)
+
+    gate_proj = gate_acc[...]
+    hidden[...] = (gate_proj / (1.0 + jnp.exp(-gate_proj)) * up_acc[...]).astype(bf16)
+
+    def ret_copy(step, r):
+        dest = lax.rem(me_d + r, dev_count)
+        return remote(
+            ret_send.at[step, dest],
+            ret_recv.at[step, me_d],
+            ret_send_sem.at[step, r],
+            ret_recv_sem.at[step, me_d],
+            me_g,
+            dest,
+        )
+
+    def col_copy(step, side):
+        dest = chunk_at(step) * 2 + side
+        return remote(
+            col_send.at[step, side],
+            col_recv.at[me_g],
+            col_send_sem.at[step, side],
+            col_recv_sem.at[me_g],
+            dest,
+            me_d,
+        )
+
+    def produce(step):
+        down_copy(step).wait()
+        result = jnp.dot(hidden[...], w_down[step], preferred_element_type=f32)
+        for s in range(dev_count):
+            for side in range(2):
+                pieces = []
+                for q in range(4):
+                    start = side * block + q * pack_width
+                    piece = result[tokens * s : tokens * (s + 1), start : start + widths[q]]
+                    if widths[q] < pack_width:
+                        piece = jnp.concatenate(
+                            [piece, jnp.zeros((tokens, pack_width - widths[q]), f32)], axis=1
+                        )
+                    pieces.append(piece)
+                ret_send[step, s, side] = jnp.concatenate(pieces, axis=0).astype(bf16)
+        for r in range(1, dev_count):
+            ret_copy(step, r).start()
+        ret_recv[step, me_d] = ret_send[step, me_d]
+
+    def consume(step):
+        for r in range(1, dev_count):
+            source = lax.rem(me_d + r, dev_count)
+            remote(
+                ret_send.at[step, source],
+                ret_recv.at[step, source],
+                ret_send_sem.at[step, r],
+                ret_recv_sem.at[step, source],
+                me_g,
+                source,
+            ).wait_recv()
+        for side in range(2):
+            g = chunk_at(step) * 2 + side
+            total = residual_pack[g]
+            moved = jnp.zeros_like(total)
+            for e in range(dev_count):
+                moved = moved + combine[e][:, :1] * ret_recv[step, e, side].astype(f32)
+            following = (total + moved).astype(bf16).astype(f32)
+            next_pack[g] = following
+            square_acc[...] += following * following
+            col_send[step, side] = (following * gain_pack[g]).astype(bf16)
+        if step < chunks - 1:
+            for side in range(2):
+                col_copy(step, side).start()
+        else:
+            other = 1 - lax.rem(me_g, 2)
+            col_copy(step, other).start()
+            col_recv[me_g] = col_send[step, lax.rem(me_g, 2)]
+
+    lag = 2
+    for step in range(chunks):
+        produce(step)
+        if step >= lag:
+            consume(step - lag)
+    for step in range(max(chunks - lag, 0), chunks):
+        consume(step)
+
+    loads[4].wait()
+    for r in range(1, group_count):
+        source = lax.rem(me_g + r, group_count)
+        remote(
+            col_send.at[0, 0],
+            col_recv.at[source],
+            col_send_sem.at[0, 0],
+            col_recv_sem.at[source],
+            source,
+            me_d,
+        ).wait_recv()
+    for g in range(group_count):
+        part = col_recv[g].astype(f32)
+        for q in range(4):
+            col32[tokens * g : tokens * (g + 1), q * pack_width : q * pack_width + widths[q]] = part[
+                tokens * q : tokens * (q + 1), : widths[q]
+            ]
+    partial = jnp.dot(col32[...].astype(bf16), w_kv[...], preferred_element_type=f32)
+    for g in range(group_count):
+        part_send[g] = partial[tokens * g : tokens * (g + 1), :]
+
+    def part_copy(r):
+        dest = lax.rem(me_g + r, group_count)
+        return remote(
+            part_send.at[dest],
+            part_recv.at[me_g],
+            part_send_sem.at[r],
+            part_recv_sem.at[me_g],
+            dest,
+            me_d,
+        )
+
+    for r in range(1, group_count):
+        part_copy(r).start()
+    part_recv[me_g] = part_send[me_g]
+
+    for g in range(group_count):
+        part = next_pack[g]
+        for q in range(4):
+            start = g * block + q * pack_width
+            next32[:, start : start + widths[q]] = part[tokens * q : tokens * (q + 1), : widths[q]]
+    out_residual[...] = next32[...].astype(bf16)
+    squares = jnp.sum(square_acc[...], axis=1, keepdims=True)
+    squares = sum(squares[tokens * q : tokens * (q + 1)] for q in range(4))
+    row_scale = lax.rsqrt(squares * (1.0 / width) + epsilon)
+
+    for r in range(1, group_count):
+        source = lax.rem(me_g + r, group_count)
+        remote(
+            part_send.at[source],
+            part_recv.at[source],
+            part_send_sem.at[r],
+            part_recv_sem.at[source],
+            source,
+            me_d,
+        ).wait_recv()
+    kv_rows = part_recv[0]
+    for g in range(1, group_count):
+        kv_rows = kv_rows + part_recv[g]
+    kv_rows = kv_rows * row_scale
+    latent = kv_rows[:, :LAT]
+    latent = (
+        latent
+        * lax.rsqrt(jnp.mean(latent * latent, axis=1, keepdims=True) + epsilon)
+        * kv_gain_ref[...].astype(f32)
+    ).astype(bf16)
+    first_half = kv_rows[:, LAT : LAT + half_width]
+    second_half = kv_rows[:, LAT + half_width :]
+    cos, sin = rope_cos[...], rope_sin[...]
+    rotated = jnp.concatenate(
+        [first_half * cos - second_half * sin, second_half * cos + first_half * sin], axis=1
+    ).astype(bf16)
+    out_entry[:, :LAT] = latent
+    out_entry[:, LAT:] = rotated
+    latent = latent.astype(f32)
+    rotated = rotated.astype(f32)
+    for t in range(tokens):
+        new_lat = latent[t : t + 1]
+        self_score = (
+            jnp.sum(q_lat[t].astype(f32) * new_lat, axis=1, keepdims=True)
+            + jnp.sum(q_rope[t].astype(f32) * rotated[t : t + 1], axis=1, keepdims=True)
+        ) * score_scale
+        old = attn_max[t]
+        largest = jnp.maximum(old, self_score)
+        shrink = jnp.exp(old - largest)
+        self_exp = jnp.exp(self_score - largest)
+        inverse = 1.0 / (attn_sum[t] * shrink + self_exp)
+        self_prob = self_exp.astype(bf16).astype(f32)
+        out_attn[t] = (
+            attn_acc[t] * (shrink * inverse) + (self_prob * inverse) * new_lat
+        ).astype(bf16)
+
+    for r in range(1, dev_count):
+        disp_copy(r).wait_send()
+        for step in range(chunks):
+            ret_copy(step, r).wait_send()
+    for step in range(chunks - 1):
+        for side in range(2):
+            col_copy(step, side).wait_send()
+    col_copy(chunks - 1, 1 - lax.rem(me_g, 2)).wait_send()
+    for r in range(1, group_count):
+        part_copy(r).wait_send()
+
+
+def fused(
+    residual,
+    routes,
+    gate_weights,
+    moe_gain,
+    attn_gain,
+    kv_gain,
+    w_gate,
+    w_up,
+    w_down,
+    w_kv,
+    q_lat,
+    q_rope,
+    cache_lat,
+    cache_rope,
+    page_table,
+    lengths,
+):
+    groups, devs = lax.axis_size("grp"), lax.axis_size("dev")
+    tokens, width = residual.shape
+    rows = tokens * devs
+    units = w_gate.shape[1]
+    chunks = groups // 2
+    block = width // groups
+    pack_width = -(-block // 512) * 128
+    k_rows = 1024 if width % 1024 == 0 else width
+    k_chunks = width // k_rows
+    kv_width = w_kv.shape[1]
+    f32, bf16 = jnp.float32, jnp.bfloat16
+    vmem = pl.BlockSpec(memory_space=pltpu.VMEM)
+    smem = pl.BlockSpec(memory_space=pltpu.SMEM)
+    hbm = pl.BlockSpec(memory_space=pl.ANY)
+    dma = pltpu.SemaphoreType.DMA
+    scratch = [
+        pltpu.VMEM((k_chunks, k_rows, units), bf16),
+        pltpu.VMEM((k_chunks, k_rows, units), bf16),
+        pltpu.VMEM((chunks, units, width // chunks), bf16),
+        pltpu.VMEM(w_kv.shape, bf16),
+        pltpu.VMEM(q_lat.shape, bf16),
+        pltpu.VMEM(q_rope.shape, bf16),
+        pltpu.VMEM(cache_lat.shape, bf16),
+        pltpu.VMEM(cache_rope.shape, bf16),
+        pltpu.VMEM((4 * tokens, width // 4), f32),
+        pltpu.VMEM((4 * tokens, width // 4), bf16),
+        pltpu.VMEM((devs, 4 * tokens, width // 4), bf16),
+        pltpu.VMEM((rows, width), f32),
+        pltpu.VMEM((k_chunks, rows, k_rows), bf16),
+        pltpu.VMEM((rows, units), f32),
+        pltpu.VMEM((rows, units), f32),
+        pltpu.VMEM((rows, units), bf16),
+        pltpu.VMEM((devs, 4 * tokens, 128), f32),
+        pltpu.VMEM((groups, 4 * tokens, pack_width), f32),
+        pltpu.VMEM((groups, 4 * tokens, pack_width), f32),
+        pltpu.VMEM((groups, 4 * tokens, pack_width), f32),
+        pltpu.VMEM((4 * tokens, pack_width), f32),
+        pltpu.VMEM((chunks, devs, 2, 4 * tokens, pack_width), bf16),
+        pltpu.VMEM((chunks, devs, 2, 4 * tokens, pack_width), bf16),
+        pltpu.VMEM((chunks, 2, 4 * tokens, pack_width), bf16),
+        pltpu.VMEM((groups, 4 * tokens, pack_width), bf16),
+        pltpu.VMEM((groups * tokens, block), f32),
+        pltpu.VMEM((groups, tokens, kv_width), f32),
+        pltpu.VMEM((groups, tokens, kv_width), f32),
+        pltpu.VMEM((tokens, HEADS, LAT), f32),
+        pltpu.VMEM((tokens, HEADS, 1), f32),
+        pltpu.VMEM((tokens, HEADS, 1), f32),
+        pltpu.VMEM((tokens, ROPE // 2), f32),
+        pltpu.VMEM((tokens, ROPE // 2), f32),
+        pltpu.VMEM((tokens, width), f32),
+        dma((5,)),
+        dma((k_chunks,)),
+        dma((k_chunks,)),
+        dma((chunks,)),
+        dma((devs,)),
+        dma((devs,)),
+        dma((chunks, devs)),
+        dma((chunks, devs)),
+        dma((chunks, 2)),
+        dma((groups,)),
+        dma((groups,)),
+        dma((groups,)),
+    ]
+    return pl.pallas_call(
+        functools.partial(fused_kernel, groups, devs),
+        out_shape=(
+            jax.ShapeDtypeStruct(residual.shape, bf16),
+            jax.ShapeDtypeStruct((tokens, kv_width), bf16),
+            jax.ShapeDtypeStruct(q_lat.shape, bf16),
+        ),
+        in_specs=[vmem] * 7 + [smem] * 2 + [hbm] * 8,
+        out_specs=(vmem, vmem, vmem),
+        scratch_shapes=scratch,
+        compiler_params=pltpu.CompilerParams(
+            collective_id=0, has_side_effects=True, vmem_limit_bytes=58 * 1024 * 1024
+        ),
+        cost_estimate=pl.CostEstimate(
+            flops=1000000000, bytes_accessed=48000000, transcendentals=200000
+        ),
+    )(
+        residual,
+        routes,
+        gate_weights,
+        moe_gain.reshape(1, -1),
+        attn_gain.reshape(1, -1),
+        kv_gain.reshape(1, -1),
+        lengths.reshape(-1, 1),
+        lengths,
+        page_table,
+        w_gate,
+        w_up,
+        w_down,
+        w_kv,
+        q_lat,
+        q_rope,
+        cache_lat,
+        cache_rope,
+    )
+
+
+def fits_fused(mesh):
+    groups, devs = mesh.shape["grp"], mesh.shape["dev"]
+    return devs == EXPERTS and groups % 2 == 0 and WIDTH % (128 * groups) == 0
+
+
 def solution(mesh):
+    body = fused if fits_fused(mesh) else local
     in_specs = (
         P(("grp", "dev"), None),
         P(("grp", "dev"), None),
@@ -167,4 +736,4 @@
         P(("grp", "dev")),
     )
     out_specs = (P(("grp", "dev"), None), P(("grp", "dev"), None), P(("grp", "dev"), None, None))
-    return jax.shard_map(local, mesh=mesh, in_specs=in_specs, out_specs=out_specs, check_vma=False)
+    return jax.shard_map(body, mesh=mesh, in_specs=in_specs, out_specs=out_specs, check_vma=False)

time: 131 us -> 51.3 us (0.39)
  the two profiles are of different devices: /device:TPU:8 before, /device:TPU:0 now
where the time goes in v1:
time: 51.3 us; the launch traced here: 50.8 us
  Pallas kernels  35.6 us (69%)
  local copies, waits for them, and re-layouts  14.6 us (28%)
  between operations  0.64 us (1%)
    pallas_call x1, Pallas kernels, fused(): pl.pallas_call(functools.partial(fused_kernel, groups, devs), out_shape=(...  35.6 us
    unnamed x6, local copies, waits for them, and re-layouts  9.36 us
    reshape x1, local copies, waits for them, and re-layouts, fused(): moe_gain.reshape(1, -1)  1.34 us
    reshape x1, local copies, waits for them, and re-layouts, fused(): attn_gain.reshape(1, -1)  1.34 us
    reshape x1, local copies, waits for them, and re-layouts, fused(): lengths.reshape(-1, 1)  1.3 us
    reshape x1, local copies, waits for them, and re-layouts, fused(): kv_gain.reshape(1, -1)  1.25 us

profile of v1, /device:TPU:0, one launch (start us, length us, event | category | flops | bytes accessed | tf_op | source)
XLA Modules:
  0.0 50.8 jit_solution(16763689784684062158)
XLA Ops:
  0.6 1.3 %copy.20.gates_ref = bf16[4,2]{1,0:T(4,128)(2,1)} copy(bf16[4,2]{0,1:T(2,128)(2,1)} %param.18) | data formatting | bytes 32 | tf_op args[2]
  1.9 1.3 %copy.19.routes_ref = s32[4,2]{1,0:T(4,128)} copy(s32[4,2]{0,1:T(2,128)} %param.17) | data formatting | bytes 64 | tf_op args[1]
  3.2 1.3 %reshape.20.kv_gain_ref = bf16[1,512]{1,0:T(2,128)(2,1)} reshape(bf16[512]{0:T(512)(128)(2,1)} %param.21) | data formatting | bytes 2048 | tf_op jit(solution)/shard_map/reshape | solution.py:698
  4.5 1.3 %copy.21.lengths_ref = s32[4,1]{1,0:T(4,128)} copy(s32[4,1]{0,1:T(1,128)} %bitcast.1) | data formatting | bytes 32 | tf_op jit(solution)/shard_map/reshape | solution.py:699
  5.8 1.3 %reshape.18.moe_gain_ref = bf16[1,7168]{1,0:T(2,128)(2,1)} reshape(bf16[7168]{0:T(1024)(128)(2,1)} %param.19) | data formatting | bytes 28672 | tf_op jit(solution)/shard_map/reshape | solution.py:696
  7.1 1.3 %reshape.19.attn_gain_ref = bf16[1,7168]{1,0:T(2,128)(2,1)} reshape(bf16[7168]{0:T(1024)(128)(2,1)} %param.20) | data formatting | bytes 28672 | tf_op jit(solution)/shard_map/reshape | solution.py:697
  8.4 2.4 %copy.22.w_kv_hbm = bf16[896,576]{1,0:T(8,128)(2,1)} copy(bf16[896,576]{0,1:T(8,128)(2,1)} %param.25) | data formatting | bytes 2064384 | tf_op args[9]
  10.8 35.6 %shard_map.175 = (bf16[4,7168]{1,0:T(4,128)(2,1)}, bf16[4,576]{1,0:T(4,128)(2,1)}, bf16[4,64,512]{2,1,0:T(8,128)(2,1)}) custom-call(bf16[4,7168]{1,0:T(4,128)(2,1)} %residual_ref.1, s32[4,2]{1,0:T(4,128)} %copy.19.routes_ref, bf16[4,2]{1,0:T(4,128)(2,1)} %copy.20.gates_ref, bf16[1,7168]{1,0:T(2,128)(2,1)} %reshape.18.moe_gain_ref, ...), custom_call_target="tpu_custom_call" | custom-call | flops 1000000000 | bytes 48000000 | tf_op jit(solution)/shard_map/pallas_call | solution.py:676
  46.4 1.5 %copy.26 = bf16[4,7168]{1,0:T(4,128)(2,1)} copy(bf16[4,7168]{1,0:T(4,128)(2,1)} %get-tuple-element.6) | data formatting | bytes 114688
  47.8 1.3 %copy.27 = bf16[4,576]{1,0:T(4,128)(2,1)} copy(bf16[4,576]{1,0:T(4,128)(2,1)} %get-tuple-element.7) | data formatting | bytes 9216
  49.1 1.7 %copy.28 = bf16[4,64,512]{2,1,0:T(8,128)(2,1)} copy(bf16[4,64,512]{2,1,0:T(8,128)(2,1)} %get-tuple-element.8) | data formatting | bytes 524288

commit v2 on v1

--- a/solution.py
+++ b/solution.py
@@ -9,6 +9,7 @@
 from jax.sharding import PartitionSpec as P
 
 WIDTH = 7168
+ATTEND_PLACES = (1, 2, 3, 4)
 HEADS = 64
 LAT = 512
 ROPE = 64
@@ -162,7 +163,6 @@
     moe_gain_ref,
     attn_gain_ref,
     kv_gain_ref,
-    lengths_ref,
     lengths_smem,
     table_smem,
     w_gate_hbm,
@@ -307,10 +307,14 @@
     moe_in = (
         residual
         * lax.rsqrt(jnp.mean(residual * residual, axis=1, keepdims=True) + epsilon)
-        * moe_gain_ref[...].astype(f32)
-    )
+    )
+    moe_gain = moe_gain_ref[...].astype(f32)
     for q in range(4):
-        pack32[tokens * q : tokens * (q + 1), :] = moe_in[:, q * quarter : (q + 1) * quarter]
+        for j in range(quarter // 128):
+            lanes = q * (quarter // 128) + j
+            pack32[tokens * q : tokens * (q + 1), j * 128 : (j + 1) * 128] = (
+                moe_in[:, lanes * 128 : (lanes + 1) * 128] * moe_gain[lanes : lanes + 1]
+            )
     packed = pack32[...].astype(bf16)
     disp_send[...] = packed
     disp_recv[me_d] = packed
@@ -328,8 +332,12 @@
 
     routes = routes_ref[...]
     gates = gates_ref[...].astype(f32)
+    diagonal = lax.broadcasted_iota(jnp.int32, (tokens, tokens), 0) == lax.broadcasted_iota(
+        jnp.int32, (tokens, tokens), 1
+    )
     for e in range(dev_count):
-        weight = jnp.sum(jnp.where(routes == e, gates, 0.0), axis=1, keepdims=True)
+        weight = jnp.sum(jnp.where(routes == e, gates, 0.0), axis=0, keepdims=True)
+        weight = jnp.sum(jnp.where(diagonal, weight, 0.0), axis=1, keepdims=True)
         weight = jnp.broadcast_to(weight, (tokens, 128))
         for q in range(4):
             combine[e, tokens * q : tokens * (q + 1), :] = weight
@@ -341,20 +349,24 @@
             rows = slice(tokens * q, tokens * (q + 1))
             start = g * block + q * pack_width
             residual_pack[g, rows, : widths[q]] = residual[:, start : start + widths[q]]
-            gain_pack[g, rows, : widths[q]] = jnp.broadcast_to(
-                attn_gain[:, start : start + widths[q]], (tokens, widths[q])
-            )
+            for j in range(widths[q] // 128):
+                lanes = start // 128 + j
+                gain_pack[g, rows, j * 128 : (j + 1) * 128] = jnp.broadcast_to(
+                    attn_gain[lanes : lanes + 1], (tokens, 128)
+                )
     square_acc[...] = jnp.zeros_like(square_acc)
     half_width = ROPE // 2
     at = lax.broadcasted_iota(jnp.int32, (tokens, half_width), 1).astype(f32)
     freqs = jnp.exp(at * (-2.0 / ROPE * math.log(10000.0)))
-    angle = lengths_ref[...].astype(f32) * freqs
+    row_at = lax.broadcasted_iota(jnp.int32, (tokens, half_width), 0)
+    lengths = jnp.zeros((tokens, half_width), jnp.int32)
+    for t in range(tokens):
+        lengths = jnp.where(row_at == t, lengths_smem[t], lengths)
+    angle = lengths.astype(f32) * freqs
     rope_cos[...] = jnp.cos(angle)
     rope_sin[...] = jnp.sin(angle)
 
-    for load in loads[:4]:
-        load.wait()
-    for t in range(tokens):
+    def attend_cached(t):
         query = q_lat[t]
         query_rope = q_rope[t]
         pages = [cache_lat[table_smem[t, p]] for p in range(PAGES_REQ)]
@@ -381,6 +393,15 @@
                 probs[:, p * PAGE : (p + 1) * PAGE], pages[p], preferred_element_type=f32
             )
         attn_acc[t] = summed
+
+    def attend_at(place):
+        for t in range(tokens):
+            if ATTEND_PLACES[t] == place:
+                attend_cached(t)
+
+    for load in loads[:4]:
+        load.wait()
+    attend_at(0)
 
     for r in range(1, dev_count):
         source = lax.rem(me_d + r, dev_count)
@@ -486,7 +507,9 @@
         if step >= lag:
             consume(step - lag)
     for step in range(max(chunks - lag, 0), chunks):
+        attend_at(1 if step < chunks - 1 else 2)
         consume(step)
+    attend_at(3)
 
     loads[4].wait()
     for r in range(1, group_count):
@@ -505,7 +528,9 @@
             col32[tokens * g : tokens * (g + 1), q * pack_width : q * pack_width + widths[q]] = part[
                 tokens * q : tokens * (q + 1), : widths[q]
             ]
-    partial = jnp.dot(col32[...].astype(bf16), w_kv[...], preferred_element_type=f32)
+    partial = lax.dot_general(
+        col32[...].astype(bf16), w_kv[...], (((1,), (1,)), ((), ())), preferred_element_type=f32
+    )
     for g in range(group_count):
         part_send[g] = partial[tokens * g : tokens * (g + 1), :]
 
@@ -523,6 +548,7 @@
     for r in range(1, group_count):
         part_copy(r).start()
     part_recv[me_g] = part_send[me_g]
+    attend_at(4)
 
     for g in range(group_count):
         part = next_pack[g]
@@ -549,10 +575,11 @@
         kv_rows = kv_rows + part_recv[g]
     kv_rows = kv_rows * row_scale
     latent = kv_rows[:, :LAT]
-    latent = (
-        latent
-        * lax.rsqrt(jnp.mean(latent * latent, axis=1, keepdims=True) + epsilon)
-        * kv_gain_ref[...].astype(f32)
+    latent = latent * lax.rsqrt(jnp.mean(latent * latent, axis=1, keepdims=True) + epsilon)
+    kv_gain = kv_gain_ref[...].astype(f32)
+    latent = jnp.concatenate(
+        [latent[:, j * 128 : (j + 1) * 128] * kv_gain[j : j + 1] for j in range(LAT // 128)],
+        axis=1,
     ).astype(bf16)
     first_half = kv_rows[:, LAT : LAT + half_width]
     second_half = kv_rows[:, LAT + half_width :]
@@ -619,7 +646,8 @@
     pack_width = -(-block // 512) * 128
     k_rows = 1024 if width % 1024 == 0 else width
     k_chunks = width // k_rows
-    kv_width = w_kv.shape[1]
+    w_kv = w_kv.T
+    kv_width = w_kv.shape[0]
     f32, bf16 = jnp.float32, jnp.bfloat16
     vmem = pl.BlockSpec(memory_space=pltpu.VMEM)
     smem = pl.BlockSpec(memory_space=pltpu.SMEM)
@@ -673,14 +701,14 @@
         dma((groups,)),
         dma((groups,)),
     ]
-    return pl.pallas_call(
+    results = pl.pallas_call(
         functools.partial(fused_kernel, groups, devs),
         out_shape=(
             jax.ShapeDtypeStruct(residual.shape, bf16),
             jax.ShapeDtypeStruct((tokens, kv_width), bf16),
             jax.ShapeDtypeStruct(q_lat.shape, bf16),
         ),
-        in_specs=[vmem] * 7 + [smem] * 2 + [hbm] * 8,
+        in_specs=[vmem] * 6 + [smem] * 2 + [hbm] * 8,
         out_specs=(vmem, vmem, vmem),
         scratch_shapes=scratch,
         compiler_params=pltpu.CompilerParams(
@@ -691,12 +719,11 @@
         ),
     )(
         residual,
-        routes,
-        gate_weights,
-        moe_gain.reshape(1, -1),
-        attn_gain.reshape(1, -1),
-        kv_gain.reshape(1, -1),
-        lengths.reshape(-1, 1),
+        routes.T,
+        gate_weights.T,
+        moe_gain.reshape(-1, 128),
+        attn_gain.reshape(-1, 128),
+        kv_gain.reshape(-1, 128),
         lengths,
         page_table,
         w_gate,
@@ -708,6 +735,18 @@
         cache_lat,
         cache_rope,
     )
+    return pl.pallas_call(
+        copy_kernel,
+        out_shape=tuple(jax.ShapeDtypeStruct(one.shape, one.dtype) for one in results),
+        in_specs=[vmem] * 3,
+        out_specs=(vmem,) * 3,
+    )(*results)
+
+
+def copy_kernel(residual_in, entry_in, attn_in, residual_out, entry_out, attn_out):
+    residual_out[...] = residual_in[...]
+    entry_out[...] = entry_in[...]
+    attn_out[...] = attn_in[...]
 
 
 def fits_fused(mesh):

time: 51.3 us -> 37.4 us (0.73)
  local copies, waits for them, and re-layouts: 14.6 us -> 0 us
  Pallas kernels: 35.6 us -> 36.6 us
    unnamed x6 -> x0, local copies, waits for them, and re-layouts: 9.36 us -> none
    reshape x4 -> x0, local copies, waits for them, and re-layouts: 5.22 us -> none  [the longest x1 1.34 us: fused(): moe_gain.reshape(1, -1)]
    pallas_call x0 -> x1, Pallas kernels: none -> 1.73 us  [fused(): pl.pallas_call(copy_kernel, out_shape=tuple((jax.ShapeDtypeStruct(one.sha...]
    pallas_call x1, Pallas kernels: 35.6 us -> 34.8 us  [fused(): pl.pallas_call(functools.partial(fused_kernel, groups, devs), out_shape=(...]
where the time goes in v2:
time: 37.4 us; the launch traced here: 37.2 us
  Pallas kernels  36.6 us (98%)
  between operations  0.65 us (2%)
    pallas_call x1, Pallas kernels, fused(): pl.pallas_call(functools.partial(fused_kernel, groups, devs), out_shape=(...  34.8 us
    pallas_call x1, Pallas kernels, fused(): pl.pallas_call(copy_kernel, out_shape=tuple((jax.ShapeDtypeStruct(one.sha...  1.73 us

profile of v2, /device:TPU:0, one launch (start us, length us, event | category | flops | bytes accessed | tf_op | source)
XLA Modules:
  0.0 37.2 jit_solution(6843066929899294748)
XLA Ops:
  0.6 34.8 %shard_map.175 = (bf16[4,7168]{1,0:T(4,128)(2,1)}, bf16[4,576]{1,0:T(4,128)(2,1)}, bf16[4,64,512]{2,1,0:T(8,128)(2,1)}) custom-call(bf16[4,7168]{1,0:T(4,128)(2,1)} %residual_ref.1, s32[2,4]{1,0:T(2,128)} %bitcast.9, bf16[2,4]{1,0:T(2,128)(2,1)} %bitcast.11, bf16[56,128]{1,0:T(8,128)(2,1)} %bitcast.7, bf16[56,128]{1,0:T(8,128)(2,1)} %bitcast.8, ...), custom_call_target="tpu_custom_call" | custom-call | flops 1000000000 | bytes 48000000 | tf_op jit(solution)/shard_map/pallas_call | solution.py:704
  35.5 1.7 %shard_map.176 = (bf16[4,7168]{1,0:T(4,128)(2,1)}, bf16[4,576]{1,0:T(4,128)(2,1)}, bf16[4,64,512]{2,1,0:T(8,128)(2,1)}) custom-call(bf16[4,7168]{1,0:T(4,128)(2,1)} %get-tuple-element.6.residual_in, bf16[4,576]{1,0:T(4,128)(2,1)} %get-tuple-element.7.entry_in, bf16[4,64,512]{2,1,0:T(8,128)(2,1)} %get-tuple-element.8.attn_in), custom_call_target="tpu_custom_call" | custom-call | tf_op jit(solution)/shard_map/pallas_call | solution.py:738

commit v3 on v2

--- a/solution.py
+++ b/solution.py
@@ -9,6 +9,7 @@
 from jax.sharding import PartitionSpec as P
 
 WIDTH = 7168
+K_STEPS = 2
 ATTEND_PLACES = (1, 2, 3, 4)
 HEADS = 64
 LAT = 512
@@ -228,7 +229,7 @@
     me_g = lax.axis_index("grp")
     me_d = lax.axis_index("dev")
     tokens, width = residual_ref.shape
-    quarter = width // 4
+    piece = width // 8
     chunks = group_count // 2
     block = width // group_count
     k_chunks, k_rows, _ = w_gate.shape
@@ -309,26 +310,34 @@
         * lax.rsqrt(jnp.mean(residual * residual, axis=1, keepdims=True) + epsilon)
     )
     moe_gain = moe_gain_ref[...].astype(f32)
-    for q in range(4):
-        for j in range(quarter // 128):
-            lanes = q * (quarter // 128) + j
-            pack32[tokens * q : tokens * (q + 1), j * 128 : (j + 1) * 128] = (
-                moe_in[:, lanes * 128 : (lanes + 1) * 128] * moe_gain[lanes : lanes + 1]
-            )
+    for half in range(2):
+        for q in range(4):
+            for j in range(piece // 128):
+                lanes = (half * 4 + q) * (piece // 128) + j
+                pack32[half, tokens * q : tokens * (q + 1), j * 128 : (j + 1) * 128] = (
+                    moe_in[:, lanes * 128 : (lanes + 1) * 128] * moe_gain[lanes : lanes + 1]
+                )
     packed = pack32[...].astype(bf16)
     disp_send[...] = packed
-    disp_recv[me_d] = packed
+    for half in range(2):
+        disp_recv[half, me_d] = packed[half]
 
     pl.semaphore_wait(barrier, dev_count - 1 + group_count - 1)
 
-    def disp_copy(r):
+    def disp_copy(half, r):
         dest = lax.rem(me_d + r, dev_count)
         return remote(
-            disp_send, disp_recv.at[me_d], disp_send_sem.at[r], disp_recv_sem.at[me_d], me_g, dest
-        )
-
-    for r in range(1, dev_count):
-        disp_copy(r).start()
+            disp_send.at[half],
+            disp_recv.at[half, me_d],
+            disp_send_sem.at[half, r],
+            disp_recv_sem.at[half, me_d],
+            me_g,
+            dest,
+        )
+
+    for half in range(2):
+        for r in range(1, dev_count):
+            disp_copy(half, r).start()
 
     routes = routes_ref[...]
     gates = gates_ref[...].astype(f32)
@@ -403,30 +412,36 @@
         load.wait()
     attend_at(0)
 
-    for r in range(1, dev_count):
-        source = lax.rem(me_d + r, dev_count)
-        remote(
-            disp_send, disp_recv.at[source], disp_send_sem.at[r], disp_recv_sem.at[source], me_g, source
-        ).wait_recv()
-    for s in range(dev_count):
-        part = disp_recv[s].astype(f32)
-        for q in range(4):
-            rows32[tokens * s : tokens * (s + 1), q * quarter : (q + 1) * quarter] = part[
-                tokens * q : tokens * (q + 1), :
-            ]
-    for k in range(k_chunks):
-        rows16[k] = rows32[:, k * k_rows : (k + 1) * k_rows].astype(bf16)
-
     gate_acc[...] = jnp.zeros_like(gate_acc)
     up_acc[...] = jnp.zeros_like(up_acc)
-
-    @pl.loop(0, k_chunks)
-    def _(k):
-        gate_copy(k).wait()
-        picked = rows16[k]
-        gate_acc[...] += jnp.dot(picked, w_gate[k], preferred_element_type=f32)
-        up_copy(k).wait()
-        up_acc[...] += jnp.dot(picked, w_up[k], preferred_element_type=f32)
+    half_chunks = k_chunks // 2
+    for half in range(2):
+        for r in range(1, dev_count):
+            source = lax.rem(me_d + r, dev_count)
+            remote(
+                disp_send.at[half],
+                disp_recv.at[half, source],
+                disp_send_sem.at[half, r],
+                disp_recv_sem.at[half, source],
+                me_g,
+                source,
+            ).wait_recv()
+        for s in range(dev_count):
+            part = disp_recv[half, s].astype(f32)
+            for q in range(4):
+                rows32[tokens * s : tokens * (s + 1), q * piece : (q + 1) * piece] = part[
+                    tokens * q : tokens * (q + 1), :
+                ]
+        for k in range(half_chunks):
+            rows16[half * half_chunks + k] = rows32[:, k * k_rows : (k + 1) * k_rows].astype(bf16)
+
+        @pl.loop(half * half_chunks, (half + 1) * half_chunks)
+        def _(k):
+            gate_copy(k).wait()
+            picked = rows16[k]
+            gate_acc[...] += jnp.dot(picked, w_gate[k], preferred_element_type=f32)
+            up_copy(k).wait()
+            up_acc[...] += jnp.dot(picked, w_up[k], preferred_element_type=f32)
 
     gate_proj = gate_acc[...]
     hidden[...] = (gate_proj / (1.0 + jnp.exp(-gate_proj)) * up_acc[...]).astype(bf16)
@@ -501,13 +516,16 @@
             col_copy(step, other).start()
             col_recv[me_g] = col_send[step, lax.rem(me_g, 2)]
 
-    lag = 2
+    lag = 4
     for step in range(chunks):
         produce(step)
         if step >= lag:
             consume(step - lag)
     for step in range(max(chunks - lag, 0), chunks):
-        attend_at(1 if step < chunks - 1 else 2)
+        if step == max(chunks - 2, 0):
+            attend_at(1)
+        if step == chunks - 1:
+            attend_at(2)
         consume(step)
     attend_at(3)
 
@@ -608,7 +626,8 @@
         ).astype(bf16)
 
     for r in range(1, dev_count):
-        disp_copy(r).wait_send()
+        for half in range(2):
+            disp_copy(half, r).wait_send()
         for step in range(chunks):
             ret_copy(step, r).wait_send()
     for step in range(chunks - 1):
@@ -644,7 +663,7 @@
     chunks = groups // 2
     block = width // groups
     pack_width = -(-block // 512) * 128
-    k_rows = 1024 if width % 1024 == 0 else width
+    k_rows = width // 2 // K_STEPS
     k_chunks = width // k_rows
     w_kv = w_kv.T
     kv_width = w_kv.shape[0]
@@ -662,10 +681,10 @@
         pltpu.VMEM(q_rope.shape, bf16),
         pltpu.VMEM(cache_lat.shape, bf16),
         pltpu.VMEM(cache_rope.shape, bf16),
-        pltpu.VMEM((4 * tokens, width // 4), f32),
-        pltpu.VMEM((4 * tokens, width // 4), bf16),
-        pltpu.VMEM((devs, 4 * tokens, width // 4), bf16),
-        pltpu.VMEM((rows, width), f32),
+        pltpu.VMEM((2, 4 * tokens, width // 8), f32),
+        pltpu.VMEM((2, 4 * tokens, width // 8), bf16),
+        pltpu.VMEM((2, devs, 4 * tokens, width // 8), bf16),
+        pltpu.VMEM((rows, width // 2), f32),
         pltpu.VMEM((k_chunks, rows, k_rows), bf16),
         pltpu.VMEM((rows, units), f32),
         pltpu.VMEM((rows, units), f32),
@@ -692,8 +711,8 @@
         dma((k_chunks,)),
         dma((k_chunks,)),
         dma((chunks,)),
-        dma((devs,)),
-        dma((devs,)),
+        dma((2, devs)),
+        dma((2, devs)),
         dma((chunks, devs)),
         dma((chunks, devs)),
         dma((chunks, 2)),

time: 37.4 us -> 35.6 us (0.952)
  Pallas kernels: 36.6 us -> 34.7 us
    pallas_call x1, Pallas kernels: 34.8 us -> 33 us  [fused(): pl.pallas_call(functools.partial(fused_kernel, groups, devs), out_shape=(...]
where the time goes in v3:
time: 35.6 us; the launch traced here: 35.4 us
  Pallas kernels  34.7 us (97%)
  between operations  0.65 us (2%)
    pallas_call x1, Pallas kernels, fused(): pl.pallas_call(functools.partial(fused_kernel, groups, devs), out_shape=(...  33 us
    pallas_call x1, Pallas kernels, fused(): pl.pallas_call(copy_kernel, out_shape=tuple((jax.ShapeDtypeStruct(one.sha...  1.73 us

profile of v3, /device:TPU:0, one launch (start us, length us, event | category | flops | bytes accessed | tf_op | source)
XLA Modules:
  0.0 35.4 jit_solution(13459085267087828333)
XLA Ops:
  0.6 33.0 %shard_map.175 = (bf16[4,7168]{1,0:T(4,128)(2,1)}, bf16[4,576]{1,0:T(4,128)(2,1)}, bf16[4,64,512]{2,1,0:T(8,128)(2,1)}) custom-call(bf16[4,7168]{1,0:T(4,128)(2,1)} %residual_ref.1, s32[2,4]{1,0:T(2,128)} %bitcast.9, bf16[2,4]{1,0:T(2,128)(2,1)} %bitcast.11, bf16[56,128]{1,0:T(8,128)(2,1)} %bitcast.7, bf16[56,128]{1,0:T(8,128)(2,1)} %bitcast.8, ...), custom_call_target="tpu_custom_call" | custom-call | flops 1000000000 | bytes 48000000 | tf_op jit(solution)/shard_map/pallas_call | solution.py:723
  33.7 1.7 %shard_map.176 = (bf16[4,7168]{1,0:T(4,128)(2,1)}, bf16[4,576]{1,0:T(4,128)(2,1)}, bf16[4,64,512]{2,1,0:T(8,128)(2,1)}) custom-call(bf16[4,7168]{1,0:T(4,128)(2,1)} %get-tuple-element.6.residual_in, bf16[4,576]{1,0:T(4,128)(2,1)} %get-tuple-element.7.entry_in, bf16[4,64,512]{2,1,0:T(8,128)(2,1)} %get-tuple-element.8.attn_in), custom_call_target="tpu_custom_call" | custom-call | tf_op jit(solution)/shard_map/pallas_call | solution.py:757
